TPU v7x, 256 devices: a whole 4x4x8 slice. The times are simulated.
256 devices in a mesh: pair: 64 (over x, z, core), aux: 4 (over y).
Axes of the slice: x: 4, y: 4, z: 8, core: 2. Of those that a mesh axis runs over, the one named last changes fastest.
Arguments:
- three_index: bfloat16 [256, 32, 32, 2048], P('pair', None, None, 'aux'), may hold values from -6 to 6
- occ_blocks: bfloat16 [64, 3, 32, 32], P('pair'), may hold values from -0.625 to 0.625
- virt_blocks: bfloat16 [64, 7, 32, 32], P('pair'), may hold values from -0.5 to 0.5
- tile_shift: int32 [64, 4], replicated, may hold values from 0 to 3, each once within a row
- tile_count: int32 [64], replicated, may hold values from 1 to 4, 128 in all
- block_owner: int32 [64], replicated, may hold values from 0 to 63, each once
Outputs:
- polarizability: float32 [2048, 2048], P('pair', 'aux')
Inputs may be any that keep to these rules, and one draw needn't show every extreme that they name: `tile_shift`: each row holds every offset once. `tile_count`: the counts sum to 128 and the largest is 4; slots at or beyond a device's count are not used. `block_owner`: every device owns exactly one block row.
All inputs are finite; a program needn't handle non-finite values.
Results may differ from a plain program's by a relative error of at most 0.0041.
Values may be sent and summed in bfloat16 or wider, within the bound.
A program may use at most 128 MiB of HBM per device.

v0:
```python
import math

import jax
import jax.numpy as jnp
from jax import lax
from jax.sharding import PartitionSpec as P

TPD = 2


def tile_tables(tile_shift, tile_count, block_owner):
    block_count = block_owner.shape[0]
    slot_count = tile_shift.shape[1]
    devices = tile_count.shape[0]
    device_ids = jnp.arange(devices, dtype=jnp.int32)
    block_ids = jnp.arange(block_count, dtype=jnp.int32)
    row_block = jnp.sum(
        jnp.where(block_owner[None, :] == device_ids[:, None], block_ids[None, :], 0), axis=1
    )
    col_block = (row_block[:, None] + tile_shift - slot_count // 2) % block_count
    slot_ids = jnp.arange(slot_count, dtype=jnp.int32)
    tile_live = slot_ids[None, :] < tile_count[:, None]
    return (row_block, col_block, tile_live)


def virtual_pairs(virt_blocks, col_block, tile_live):
    block_count = virt_blocks.shape[0]
    centre = (virt_blocks.shape[1] - 1) // 2
    offset = (col_block[:, None, :] - col_block[:, :, None]) % block_count
    offset = jnp.where(offset > block_count // 2, offset - block_count, offset) + centre
    chosen = virt_blocks[col_block[:, :, None], offset]
    return jnp.where(tile_live[:, None, :, None, None], chosen, jnp.zeros((), virt_blocks.dtype))


def occupied_sources(row_block, col_block, tile_live, block_owner):
    block_count = block_owner.shape[0]
    slot_count = col_block.shape[1]
    slot_ids = jnp.arange(slot_count, dtype=jnp.int32)
    source_list = []
    found_list = []
    for neighbour in range(3):
        near_block = (row_block + neighbour - 1) % block_count
        owner_device = block_owner[near_block]
        near_cols = col_block[owner_device]
        near_live = tile_live[owner_device]
        matches = (near_cols[:, None, :] == col_block[:, :, None]) & near_live[:, None, :]
        present = jnp.any(matches, axis=2) & tile_live
        position_in = jnp.sum(jnp.where(matches, slot_ids[None, None, :], 0), axis=2)
        source_list.append(owner_device[:, None] * slot_count + position_in)
        found_list.append(present)
    return (jnp.stack(source_list, axis=2), jnp.stack(found_list, axis=2))


def per_device(three_index, occ_blocks, virt_blocks, tile_shift, tile_count, block_owner):
    pairs_n = lax.axis_size("pair")
    position = lax.axis_index("pair")
    slot_count = three_index.shape[0]
    tile_width = three_index.shape[1]
    col_local = three_index.shape[3]
    piece_width = tile_width * col_local // pairs_n
    tile_total = pairs_n * slot_count
    occ_all, virt_all = (
        lax.all_gather(occ_blocks, "pair", axis=0, tiled=True),
        lax.all_gather(virt_blocks, "pair", axis=0, tiled=True),
    )
    row_block, col_block, tile_live = tile_tables(tile_shift, tile_count, block_owner)
    own_cols = lax.dynamic_index_in_dim(col_block, position, 0, keepdims=True)
    own_live = lax.dynamic_index_in_dim(tile_live, position, 0, keepdims=True)
    virt_pairs = virtual_pairs(virt_all, own_cols, own_live)[0]
    half_virt = jnp.einsum(
        "jksv,kmvq->jmsq", virt_pairs, three_index, preferred_element_type=jnp.float32
    )
    half_virt = half_virt.astype(jnp.bfloat16).reshape(slot_count, tile_width, pairs_n, piece_width)
    sources, valid = occupied_sources(row_block, col_block, tile_live, block_owner)
    sources = sources.reshape(tile_total, 3)
    valid = valid.reshape(tile_total, 3)
    occ_rows = jnp.where(
        valid[:, :, None, None],
        occ_all[jnp.repeat(row_block, slot_count)],
        jnp.zeros((), occ_all.dtype),
    )
    target_live = tile_live.reshape(tile_total)
    sources_flat = lax.all_to_all(half_virt, "pair", split_axis=2, concat_axis=0, tiled=True)[
        :, :, 0, :
    ]
    summed = jnp.zeros(sources_flat.shape, jnp.float32)
    for neighbour in range(3):
        summed = summed + jnp.einsum(
            "tlm,tmx->tlx",
            occ_rows[:, neighbour],
            sources_flat[sources[:, neighbour]],
            preferred_element_type=jnp.float32,
        )
    masked = jnp.where(target_live[:, None, None], summed, 0.0)
    full_virt = masked.astype(jnp.bfloat16)[:, :, None, :]
    returned = lax.all_to_all(full_virt, "pair", split_axis=0, concat_axis=2, tiled=True)
    returned_view = returned.reshape(slot_count, tile_width, tile_width, col_local)
    partial_value = jnp.einsum(
        "tmsp,tmsq->pq",
        lax.all_gather(three_index, "aux", axis=3, tiled=True),
        returned_view,
        preferred_element_type=jnp.float32,
    )
    scale_factor = 1.0 / math.sqrt(tile_width * tile_width * pairs_n * TPD)
    summed_all = lax.psum(partial_value, "pair")
    row_share = summed_all.shape[0] // pairs_n
    polarizability = lax.dynamic_slice_in_dim(summed_all, position * row_share, row_share, 0)
    return polarizability * scale_factor


def solution(mesh):
    in_specs = (
        P("pair", None, None, "aux"),
        P("pair", None, None, None),
        P("pair", None, None, None),
        P(),
        P(),
        P(),
    )
    out_specs = P("pair", "aux")
    return jax.shard_map(
        per_device, mesh=mesh, in_specs=in_specs, out_specs=out_specs, check_vma=False
    )
```

profile of v0, /device:TPU:8, one launch (start us, length us, event | category | flops | bytes accessed | tf_op | source)
XLA Modules:
  0.0 614.2 jit_solution(2122320318319273700)
XLA Ops:
  6.5 4.8 copy.83
  12.5 59.5 %all_gather.10 = bf16[64,7,32,32]{3,2,1,0:T(8,128)(2,1)} all-gather(bf16[1,7,32,32]{3,2,1,0:T(8,128)(2,1)S(1)} %copy-done.3), channel_id=1, replica_groups=mesh['pair'=64,'aux'=4] {'pair'}, dimensions={0}, use_global_device_ids=true | all-gather | bytes 931840 | tf_op jit(solution)/shard_map/all_gather | solution.py:64
  72.0 2.7 gather_fusion.10
  74.8 5.5 fusion.1
  80.3 7.1 %reshape.620 = bf16[4,32,64,256]{3,2,1,0:T(8,128)(2,1)} reshape(bf16[4,32,32,512]{3,2,1,0:T(8,128)(2,1)} %fusion.1) | data formatting | bytes 8388608 | tf_op jit(solution)/shard_map/reshape | solution.py:73
  87.4 6.6 %copy.84 = bf16[4,32,64,256]{3,1,0,2:T(8,128)(2,1)} copy(bf16[4,32,64,256]{3,2,1,0:T(8,128)(2,1)} %reshape.620) | data formatting | bytes 8388608 | tf_op jit(solution)/shard_map/reshape | solution.py:73
  94.0 7.1 %all-to-all-start = ((bf16[4,32,64,256]{3,1,0,2:T(8,128)(2,1)}), bf16[4,32,64,256]{3,1,0,2:T(8,128)(2,1)}, u32[]{:S(2)}, u32[]{:S(2)}) async-start(bf16[4,32,64,256]{3,1,0,2:T(8,128)(2,1)} %copy.84), calls=%async_computation | async-start | bytes 8388608 | tf_op jit(solution)/shard_map/all_to_all | solution.py:83
  101.3 0.8 gather_fusion.6
  105.3 0.8 gather_fusion.3
  110.0 127.4 %all_gather.9 = bf16[64,3,32,32]{3,2,1,0:T(8,128)(2,1)S(1)} all-gather(bf16[1,3,32,32]{3,2,1,0:T(8,128)(2,1)S(1)} %copy-done.4), channel_id=1, replica_groups=mesh['pair'=64,'aux'=4] {'pair'}, dimensions={0}, use_global_device_ids=true | all-gather | bytes 399360 | tf_op jit(solution)/shard_map/all_gather | solution.py:63
  237.4 4.0 gather_fusion.9
  241.5 6.9 %copy_select_fusion = bf16[256,3,32,32]{3,2,0,1:T(8,128)(2,1)} fusion(bf16[256,3,32,32]{3,2,1,0:T(8,128)(2,1)} %gather_fusion.9, pred[256,3]{0,1:T(4,128)(4,1)S(1)} %add_bitcast_fusion.1), kind=kLoop, calls=%fused_computation.16 | loop fusion | flops 786432 | bytes 3146496 | tf_op jit(solution)/shard_map/jit(_where)/select_n | solution.py:77
  248.4 4.9 gather_fusion.11
  253.4 5.0 gather_fusion.12
  258.3 5.0 gather_fusion.13
  263.3 4.2 fusion.7
  267.6 6.2 %fusion.6 = f32[256,32,256]{2,1,0:T(8,128)} fusion(bf16[256,32,256]{2,1,0:T(8,128)(2,1)S(1)} %copy-done.1, bf16[256,3,32,32]{3,2,0,1:T(8,128)(2,1)} %copy_select_fusion), kind=kOutput, calls=%fused_computation.25 | convolution fusion | flops 134217728 | bytes 14680064 | tf_op jit(solution)/shard_map/tlm,tmx->tlx/dot_general | solution.py:88
  273.8 7.5 %fusion = bf16[256,32,1,256]{3,1,2,0:T(8,128)(2,1)} fusion(f32[256,32,256]{2,1,0:T(8,128)S(1)} %fusion.7, f32[256,32,256]{2,1,0:T(8,128)} %fusion.6, pred[256]{0:T(512)(128)(4,1)S(1)} %lt.207, bf16[256,32,256]{2,1,0:T(8,128)(2,1)S(1)} %copy-done.2, bf16[256,3,32,32]{3,2,0,1:T(8,128)(2,1)} %copy_select_fusion), kind=kOutput, calls=%fused_computation.17 | convolution fusion | flops 142606336 | bytes 27263232 | tf_op jit(solution)/shard_map/tlm,tmx->tlx/dot_general | solution.py:88
  281.2 105.2 %all_to_all.30 = bf16[256,32,1,256]{3,1,2,0:T(8,128)(2,1)S(1)} all-to-all(bf16[256,32,1,256]{3,1,2,0:T(8,128)(2,1)} %fusion), channel_id=1, replica_groups=mesh['pair'=64,'aux'=4] {'pair'}, dimensions={0} | all-to-all | bytes 8388608 | tf_op jit(solution)/shard_map/all_to_all | solution.py:96
  386.4 4.4 copy.103
  390.8 7.1 %reshape.621 = bf16[4,32,32,512]{3,2,0,1:T(8,128)(2,1)} reshape(bf16[4,32,64,1,256]{4,2,0,1,3:T(8,128)(2,1)} %bitcast.107) | data formatting | bytes 8388608 | tf_op jit(solution)/shard_map/reshape | solution.py:97
  397.9 15.0 %convolution_bitcast_fusion = f32[2048,512]{1,0:T(8,128)} fusion(bf16[4,32,32,512]{3,2,0,1:T(8,128)(2,1)} %reshape.621, bf16[4,32,32,2048]{3,2,0,1:T(8,128)(2,1)} %all-gather.2.cloned.1.call-done), kind=kOutput, calls=%fused_computation.22 | convolution fusion | flops 8589934592 | bytes 25165824 | tf_op jit(solution)/shard_map/tmsp,tmsq->pq/dot_general | solution.py:98
  412.9 192.9 %all-reduce.2.cloned.1.call-done = f32[2048,512]{1,0:T(8,128)} async-done(((f32[2048,512]{1,0:T(8,128)}), f32[2048,512]{1,0:T(8,128)}) %all-reduce.2.cloned.1.call-update) | async-done | bytes 4194320 | tf_op jit(solution)/shard_map/psum | solution.py:105
  605.9 1.5 dynamic-slice_multiply_fusion
  (91 shorter events, 8.5 us)
Async XLA Ops:
  6.5 391.4 %all-gather.2.cloned.1.call-start = ((), (), s32[]{:S(2)}) async-start(), calls=%async_computation.2 | async-start | bytes 20971520 | tf_op jit(solution)/shard_map/all_gather | solution.py:100
  11.3 0.7 copy-start
  11.3 0.8 copy-start.6
  11.3 1.2 copy-start.3
  11.3 63.4 %copy-start.5 = (s32[64]{0:T(128)S(1)}, s32[64]{0:T(128)}, u32[]{:S(2)}) copy-start(s32[64]{0:T(128)} %param.10) | copy-start | bytes 772
  94.0 16.0 %copy-start.4 = (bf16[1,3,32,32]{3,2,1,0:T(8,128)(2,1)S(1)}, bf16[1,3,32,32]{3,2,1,0:T(8,128)(2,1)}, u32[]{:S(2)}) copy-start(bf16[1,3,32,32]{3,2,1,0:T(8,128)(2,1)} %param.7) | copy-start | bytes 18436
  94.0 154.4 %all-to-all-start = ((bf16[4,32,64,256]{3,1,0,2:T(8,128)(2,1)}), bf16[4,32,64,256]{3,1,0,2:T(8,128)(2,1)}, u32[]{:S(2)}, u32[]{:S(2)}) async-start(bf16[4,32,64,256]{3,1,0,2:T(8,128)(2,1)} %copy.84), calls=%async_computation | async-start | bytes 8388608 | tf_op jit(solution)/shard_map/all_to_all | solution.py:83
  101.1 504.7 %all-reduce.2.cloned.1.call-start = ((), (), s32[]{:S(2)}) async-start(), calls=%async_computation.3 | async-start | bytes 8388608 | tf_op jit(solution)/shard_map/psum | solution.py:105
  263.3 4.2 copy-start.1
  267.6 6.2 %copy-start.2 = (bf16[256,32,256]{2,1,0:T(8,128)(2,1)S(1)}, bf16[256,32,256]{2,1,0:T(8,128)(2,1)}, u32[]{:S(2)}) copy-start(bf16[256,32,256]{2,1,0:T(8,128)(2,1)} %gather_fusion.13) | copy-start | bytes 12582916
Sparse Core Ops, SparseCore 0:
  11.4 159.4 all-gather.1
  413.0 192.7 all-reduce.1
where the time goes:
time: 615 us; the launch traced here: 614 us
  blocking collectives  292 us (47%)
  waiting for transfers between devices  193 us (31%)
  local copies, waits for them, and re-layouts  60.9 us (10%)
  matrix products  38.4 us (6%)
  between operations  13.7 us (2%)
  other arithmetic  8.95 us (1%)
  starting transfers between devices  7.17 us (1%)
    psum x1, waiting for transfers between devices, per_device(): summed_all = lax.psum(partial_value, 'pair')  193 us
    all_gather x1, blocking collectives, per_device(): lax.all_gather(occ_blocks, 'pair', axis=0, tiled=True)  127 us
    all_to_all x1, blocking collectives, per_device(): lax.all_to_all(full_virt, 'pair', split_axis=0, concat_axis=2, tiled=True)  105 us
    all_gather x1, blocking collectives, per_device(): lax.all_gather(virt_blocks, 'pair', axis=0, tiled=True)  59.5 us
    dot_general x3, matrix products, per_device(): jnp.einsum('tlm,tmx->tlx', occ_rows[:, neighbour], sources_flat[sources[:...  17.8 us
    dot_general x1, matrix products, per_device(): jnp.einsum('tmsp,tmsq->pq', lax.all_gather(three_index, 'aux', axis=3, ti...  15 us
    gather x3, local copies, waits for them, and re-layouts, per_device(): sources_flat[sources[:, neighbour]]  14.9 us
    reshape x2, local copies, waits for them, and re-layouts, per_device(): half_virt.astype(jnp.bfloat16)  13.7 us
  transfers between devices with their start and end apart: 3, of which 1 were waited for; matrix products, arithmetic and copies ran while one was open for 14% of the time, Pallas kernels for 0%

commit v1 on v0

v1 whole, which is shorter than its diff:
```python
import functools
import math

import jax
import jax.numpy as jnp
from jax import lax
from jax.experimental import pallas as pl
from jax.experimental.pallas import tpu as pltpu
from jax.sharding import PartitionSpec as P

NX, NY, NZ = 4, 4, 8
NG = 2 * NX
W = 4
TB = 32
HB = TB // 2
QL = 512
QH = QL // 2
LIVE = 128
RANKS = NG * NZ
MESH = pl.DeviceIdType.MESH
BF, F32 = jnp.bfloat16, jnp.float32


def tables(tile_shift, tile_count, block_owner):
    pairs = RANKS
    ids = jnp.arange(pairs, dtype=jnp.int32)
    row_block = jnp.sum(jnp.where(block_owner[None, :] == ids[:, None], ids[None, :], 0), axis=1)

    def by_plane(a):
        return a.reshape((NX, NZ, 2) + a.shape[1:]).swapaxes(0, 1).reshape((NZ, NG) + a.shape[1:])

    count = by_plane(tile_count)
    shift = by_plane(tile_shift)
    row = by_plane(row_block)
    before = (jnp.arange(NG)[None, :] < jnp.arange(NG)[:, None]).astype(jnp.int32)
    in_plane = jnp.sum(count[:, None, :] * before[None], axis=2)
    plane_total = jnp.sum(count, axis=1)
    before_z = (jnp.arange(NZ)[None, :] < jnp.arange(NZ)[:, None]).astype(jnp.int32)
    plane_start = jnp.sum(plane_total[None, :] * before_z, axis=1)
    slot = jnp.arange(W, dtype=jnp.int32)
    live = slot[None, None, :] < count[:, :, None]
    place = in_plane[:, :, None] + slot
    packed = jnp.arange(NZ, dtype=jnp.int32)[:, None, None] * 32 + place
    rank = plane_start[:, None, None] + place

    k = jnp.arange(32, dtype=jnp.int32)
    hit = (place[:, None] == k[None, :, None, None]) & live[:, None]
    g4 = jnp.arange(NG, dtype=jnp.int32)[:, None] * W
    list_t = jnp.sum(jnp.where(hit, (g4 + slot)[None, None], 0), axis=(2, 3))
    list_h = jnp.sum(jnp.where(hit, (g4 + shift)[:, None], 0), axis=(2, 3))
    first = jnp.where(k[None, :] < plane_total[:, None], 0, shift[:, 0, 0][:, None])
    list_h = list_h + first

    key = (row[:, :, None] * W + shift).reshape(-1)
    live_f = live.reshape(-1)
    packed_f = packed.reshape(-1)
    r = jnp.arange(LIVE, dtype=jnp.int32)
    by_rank = (rank.reshape(-1)[None, :] == r[:, None]) & live_f[None, :]
    rank_packed = jnp.sum(jnp.where(by_rank, packed_f[None], 0), axis=1)
    rank_key = jnp.sum(jnp.where(by_rank, key[None], 0), axis=1)
    mu = rank_key // W
    w = rank_key % W
    near = jnp.arange(3, dtype=jnp.int32) - 1
    near_w = w[:, None] - near
    near_key = (mu[:, None] + near) % RANKS * W + near_w
    match = (near_key[:, :, None] == key) & live_f & ((near_w >= 0) & (near_w < W))[:, :, None]
    found = jnp.sum(jnp.where(match, packed_f + 1, 0), axis=2)
    source = jnp.where(found > 0, found - 1, rank_packed[:, None])
    valid = (found > 0).astype(jnp.int32)

    def block_place(b):
        return (2 * (b // (2 * NZ)) + b % 2) * NZ + b // 2 % NZ

    return (
        row_block,
        list_t,
        list_h,
        rank_packed,
        block_place(mu),
        source.reshape(-1),
        valid.reshape(-1),
        block_place,
    )


def kernel(
    cap,
    list_t,
    list_h,
    rank_at,
    rank_row,
    rank_src,
    rank_ok,
    own_tab,
    tnat_h,
    tsm_h,
    comb_h,
    out,
    tnat,
    comb,
    hs,
    hbuf,
    txr0, txr1, txr2, txr3, txr4, txr5, txr6, txr7,
    hxr0, hxr1, hxr2, hxr3, hxr4, hxr5, hxr6, hxr7,
    tc,
    hc,
    tz,
    hz,
    at,
    fbuf,
    frecv,
    pbuf,
    prx,
    rxs,
    rxr,
    rzs,
    rzr,
    sems,
    txr_s,
    tzr_s,
    hxr_s,
    hzr_s,
    ys_s,
    yr_s,
    cs_s,
    cr_s,
    loc_s,
    own_s,
    out_s,
):
    txr = (txr0, txr1, txr2, txr3, txr4, txr5, txr6, txr7)
    hxr = (hxr0, hxr1, hxr2, hxr3, hxr4, hxr5, hxr6, hxr7)
    pi = lax.axis_index("pair")
    y = lax.axis_index("aux")
    c = pi % 2
    z = pi // 2 % NZ
    x = pi // (2 * NZ)
    g = 2 * x + c

    def dev_g(gg):
        return ((gg // 2 * NZ + z) * 2 + gg % 2, y)

    def dev_z(zz):
        return ((x * NZ + zz) * 2 + c, y)

    yp, ym = (y + 1) % NY, (y + NY - 1) % NY
    core = dev_g(g + 1 - 2 * c)

    def remote(src, dst, send, recv, device):
        return pltpu.make_async_remote_copy(
            src_ref=src, dst_ref=dst, send_sem=send, recv_sem=recv, device_id=device, device_id_type=MESH
        )

    def wait_bytes(ref, sem):
        pltpu.make_async_copy(ref, ref, sem).wait()

    barrier = pltpu.get_barrier_semaphore()
    for i in range(1, NG):
        pl.semaphore_signal(barrier, inc=1, device_id=dev_g((g + i) % NG), device_id_type=MESH)
    for i in range(1, NZ):
        pl.semaphore_signal(barrier, inc=1, device_id=dev_z((z + i) % NZ), device_id_type=MESH)
    pl.semaphore_signal(barrier, inc=1, device_id=(pi, yp), device_id_type=MESH)
    pl.semaphore_signal(barrier, inc=1, device_id=(pi, ym), device_id_type=MESH)

    own_t, own_h = [], []
    for k in range(NZ):
        zb = (z + 4 + k) % NZ
        own_t.append(
            pltpu.make_async_copy(
                tsm_h.at[x * NZ + zb, :, pl.ds(HB * c, HB), :], txr[k].at[pl.ds(W * g, W)], own_s.at[k]
            )
        )
        own_t[k].start()
    nat = pltpu.make_async_copy(tnat_h, tnat, loc_s.at[1])
    nat.start()
    own_c = pltpu.make_async_copy(comb_h, comb.at[g * NZ + z], loc_s.at[2])
    own_c.start()
    pl.semaphore_wait(barrier, NG + NZ)

    for i in range(1, NZ):
        remote(comb_h, comb.at[g * NZ + z], cs_s.at[0], cr_s.at[0], dev_z((z + i) % NZ)).start()

    for k in range(NZ):
        zb = (z + 4 + k) % NZ
        for i in range(1, NG):
            gg = (g + i) % NG
            remote(
                tsm_h.at[gg // 2 * NZ + zb, :, pl.ds(HB * (gg % 2), HB), :],
                txr[k].at[pl.ds(W * g, W)],
                out_s.at[k],
                txr_s.at[k],
                dev_g(gg),
            ).start()

    own_c.wait()
    wait_bytes(comb.at[pl.ds(0, NZ - 1)], cr_s.at[0])
    for i in range(1, NX):
        remote(
            comb.at[pl.ds(g * NZ, NZ)], comb.at[pl.ds(g * NZ, NZ)], cs_s.at[1], cr_s.at[1], dev_g((g + 2 * i) % NG)
        ).start()
    remote(comb.at[pl.ds(g * NZ, NZ)], comb.at[pl.ds(g * NZ, NZ)], cs_s.at[1], cr_s.at[1], core).start()
    wait_bytes(comb.at[pl.ds(0, NX * NZ)], cr_s.at[1])
    for i in range(1, NX):
        gg = (g + 2 * i) % NG
        remote(comb.at[pl.ds(gg * NZ, NZ)], comb.at[pl.ds(gg * NZ, NZ)], cs_s.at[2], cr_s.at[2], core).start()

    def t_step(k):
        zb = (z + 4 + k) % NZ
        own_t[k].wait()
        wait_bytes(txr[k].at[pl.ds(0, (NG - 1) * W)], txr_s.at[k])
        if k == 4:

            @pl.loop(0, cap)
            def _(i):
                tz[z, i] = txr[k][list_t[i]]

        else:

            @pl.loop(0, cap)
            def _(i):
                tc[zb, i] = txr[k][list_t[i]]

            remote(tc.at[zb], tz.at[z], sems.at[1], tzr_s.at[z], dev_z(zb)).start()

    for k in range(4):
        t_step(k)

    wait_bytes(comb.at[pl.ds(0, (NX - 1) * NZ)], cr_s.at[2])
    nat.wait()
    lane = lax.broadcasted_iota(jnp.int32, (TB, W * TB), 1) // TB
    keep = lane < 0
    for kk in range(W):
        keep = keep | ((lane == kk) & (own_tab[W + kk] > 0))
    rows = []
    for ww in range(W):
        band = comb[own_tab[ww], :, 0:256].astype(F32)
        band = pltpu.roll(band, (256 - TB * (W - 1 - ww)) % 256, 1)[:, : W * TB]
        rows.append(jnp.where(keep, band, 0.0).astype(BF))
    vmat = jnp.concatenate(rows, axis=0)
    slots = [own_tab[2 * W + ww] for ww in range(W)]

    for qh in range(2):

        @pl.loop(0, 2)
        def _(mh):
            @pl.loop(0, HB)
            def _(mi):
                rhs = jnp.concatenate(
                    [tnat[slots[ww], mh * HB + mi, :, qh * QH : (qh + 1) * QH] for ww in range(W)], axis=0
                )
                hs[mi] = jnp.dot(vmat, rhs, preferred_element_type=F32)

            for ww in range(W):

                @pl.loop(0, TB // 8)
                def _(sb):
                    part = hs[:, pl.ds(ww * TB + sb * 8, 8), :]
                    hbuf[qh, pl.ds(sb * 8, 8), ww, pl.ds(mh * HB, HB), :] = jnp.swapaxes(part, 0, 1).astype(BF)

    for k in range(NZ):
        zb = (z + 4 + k) % NZ
        own_h.append(pltpu.make_async_copy(hbuf.at[c, x * NZ + zb], hxr[k].at[pl.ds(W * g, W)], own_s.at[NZ + k]))
        own_h[k].start()
        for i in range(1, NG):
            gg = (g + i) % NG
            remote(
                hbuf.at[gg % 2, gg // 2 * NZ + zb], hxr[k].at[pl.ds(W * g, W)], out_s.at[NZ + k], hxr_s.at[k], dev_g(gg)
            ).start()

    for k in range(4, NZ):
        t_step(k)

    def h_step(k):
        zb = (z + 4 + k) % NZ
        own_h[k].wait()
        wait_bytes(hxr[k].at[pl.ds(0, (NG - 1) * W)], hxr_s.at[k])
        if k == 4:

            @pl.loop(0, cap)
            def _(i):
                hz[z, i] = hxr[k][list_h[i]]

        else:

            @pl.loop(0, cap)
            def _(i):
                hc[zb, i] = hxr[k][list_h[i]]

            remote(hc.at[zb], hz.at[z], sems.at[3], hzr_s.at[z], dev_z(zb)).start()

    h_step(0)
    h_step(1)

    for i in range(1, NZ):
        zz = (z + i) % NZ
        wait_bytes(tz.at[zz], tzr_s.at[zz])

    @pl.loop(0, LIVE // 8)
    def _(b):
        tiles = []
        for i in range(8):
            p = rank_at[b * 8 + i]
            tiles.append(tz[p // 32, p % 32])
        at[y, :, pl.ds(b * 128, 128)] = jnp.concatenate(tiles, axis=0).T

    lo, hi = pl.ds(0, QH), pl.ds(QH, QH)
    remote(at.at[y, lo], at.at[y, lo], ys_s.at[0], yr_s.at[0], (pi, yp)).start()
    remote(at.at[y, hi], at.at[y, hi], ys_s.at[1], yr_s.at[1], (pi, ym)).start()
    remote(at.at[y, hi], at.at[y, hi], ys_s.at[2], yr_s.at[2], (pi, yp)).start()
    remote(at.at[y, lo], at.at[y, lo], ys_s.at[3], yr_s.at[3], (pi, ym)).start()

    for k in range(2, 6):
        h_step(k)
    wait_bytes(at.at[ym, lo], yr_s.at[0])
    remote(at.at[ym, lo], at.at[ym, lo], ys_s.at[4], yr_s.at[4], (pi, yp)).start()
    wait_bytes(at.at[yp, hi], yr_s.at[1])
    remote(at.at[yp, hi], at.at[yp, hi], ys_s.at[5], yr_s.at[5], (pi, ym)).start()
    for k in range(6, NZ):
        h_step(k)

    for i in range(1, NZ):
        zz = (z + i) % NZ
        wait_bytes(hz.at[zz], hzr_s.at[zz])
    lane3 = lax.broadcasted_iota(jnp.int32, (TB, 3 * TB), 1) // TB

    @pl.loop(0, LIVE)
    def _(t):
        occ = comb[rank_row[t], :, 256 : 256 + 3 * TB]
        src, use = [], lane3 < 0
        for r in range(3):
            p = rank_src[3 * t + r]
            src.append(hz[p // 32, p % 32])
            use = use | ((lane3 == r) & (rank_ok[3 * t + r] > 0))
        occ = jnp.where(use, occ.astype(F32), 0.0).astype(BF)
        f = jnp.dot(occ, jnp.concatenate(src, axis=0), preferred_element_type=F32).astype(BF)
        fbuf[0, t] = f[:HB]
        fbuf[1, t] = f[HB:]

    swap = remote(fbuf.at[1 - c], frecv, sems.at[4], sems.at[5], core)
    swap.start()
    for i, ref in ((2, at.at[ym, hi]), (3, at.at[yp, lo]), (4, at.at[(y + 2) % NY, lo]), (5, at.at[(y + 2) % NY, hi])):
        wait_bytes(ref, yr_s.at[i])
    swap.wait_recv()

    own_q = pl.ds(pl.multiple_of(c * QH, QH), QH)
    far_q = pl.ds(pl.multiple_of((1 - c) * QH, QH), QH)

    def core_sum(i):
        xb = (x + 1 + i) % NX
        wait_bytes(prx.at[i], sems.at[8 + i])
        return pbuf[xb, :, c] + prx[i]

    def ship(i):
        xb = (x + 1 + i) % NX
        rxs[i] = core_sum(i).astype(BF)
        remote(rxs.at[i], rxr.at[i], sems.at[12 + i], sems.at[15 + i], dev_g(2 * xb + c)).start()

    for i in range(NX):
        xb = (x + 1 + i) % NX

        @pl.loop(0, 4)
        def _(mt):
            lhs = at[xb, pl.ds(mt * 128, 128), :]
            own = jnp.dot(lhs, fbuf[c].reshape(LIVE * HB, QH), preferred_element_type=F32)
            far = jnp.dot(lhs, frecv[...].reshape(LIVE * HB, QH), preferred_element_type=F32)
            pbuf[xb, pl.ds(mt * 2, 2), :, :, own_q] = own.reshape(2, 2, TB, QH)
            pbuf[xb, pl.ds(mt * 2, 2), :, :, far_q] = far.reshape(2, 2, TB, QH)

        remote(pbuf.at[xb, :, 1 - c], prx.at[i], sems.at[18 + i], sems.at[8 + i], core).start()
        if i > 0:
            ship(i - 1)

    total = core_sum(NX - 1)
    for i in range(NX - 1):
        wait_bytes(rxr.at[i], sems.at[15 + i])
        total = total + rxr[i].astype(F32)
    rzs[...] = total.astype(BF)
    for i in range(1, NZ):
        zz = (z + i) % NZ
        remote(rzs.at[zz], rzr.at[z], sems.at[6], sems.at[7], dev_z(zz)).start()
    rzr[z] = rzs[z]
    wait_bytes(rzs.at[pl.ds(0, NZ - 1)], sems.at[7])
    final = rzr[0].astype(F32)
    for zz in range(1, NZ):
        final = final + rzr[zz].astype(F32)
    out[...] = final * (1.0 / math.sqrt(TB * TB * LIVE))

    wait_bytes(comb.at[pl.ds(0, NZ - 1)], cs_s.at[0])
    wait_bytes(comb.at[pl.ds(0, NX * NZ)], cs_s.at[1])
    wait_bytes(comb.at[pl.ds(0, (NX - 1) * NZ)], cs_s.at[2])
    for k in range(NZ):
        wait_bytes(txr[k].at[pl.ds(0, (NG - 1) * W)], out_s.at[k])
    wait_bytes(tc.at[pl.ds(0, NZ - 1)], sems.at[1])
    for k in range(NZ):
        wait_bytes(hxr[k].at[pl.ds(0, (NG - 1) * W)], out_s.at[NZ + k])
    wait_bytes(hc.at[pl.ds(0, NZ - 1)], sems.at[3])
    swap.wait_send()
    wait_bytes(rzs.at[pl.ds(0, NZ - 1)], sems.at[6])
    for i in range(6):
        wait_bytes(at.at[y, lo], ys_s.at[i])
    for i in range(NX - 1):
        wait_bytes(rxs.at[i], sems.at[12 + i])
    for i in range(NX):
        wait_bytes(prx.at[i], sems.at[18 + i])


def fused(cap, cid, tabs, tnat, tsm, comb):
    smem = pl.BlockSpec(memory_space=pltpu.SMEM)
    hbm = pl.BlockSpec(memory_space=pl.ANY)
    dma = pltpu.SemaphoreType.DMA
    return pl.pallas_call(
        functools.partial(kernel, cap),
        out_shape=jax.ShapeDtypeStruct((TB, QL), F32),
        in_specs=[smem] * 7 + [hbm] * 3,
        out_specs=pl.BlockSpec(memory_space=pltpu.VMEM),
        scratch_shapes=[
            pltpu.VMEM((W, TB, TB, QL), BF),
            pltpu.VMEM((RANKS, TB, 384), BF),
            pltpu.VMEM((HB, W * TB, QH), F32),
            pltpu.VMEM((2, TB, W, TB, QH), BF),
        ]
        + [pltpu.VMEM((NG * W, HB, QL), BF)] * NZ
        + [pltpu.VMEM((NG * W, TB, QH), BF)] * NZ
        + [
            pltpu.VMEM((NZ, cap, HB, QL), BF),
            pltpu.VMEM((NZ, cap, TB, QH), BF),
            pltpu.VMEM((NZ, cap, HB, QL), BF),
            pltpu.VMEM((NZ, cap, TB, QH), BF),
            pltpu.VMEM((NY, QL, LIVE * HB), BF),
            pltpu.VMEM((2, LIVE, HB, QH), BF),
            pltpu.VMEM((LIVE, HB, QH), BF),
            pltpu.VMEM((NX, NZ, 2, TB, QL), F32),
            pltpu.VMEM((NX, NZ, TB, QL), F32),
            pltpu.VMEM((NX - 1, NZ, TB, QL), BF),
            pltpu.VMEM((NX - 1, NZ, TB, QL), BF),
            pltpu.VMEM((NZ, TB, QL), BF),
            pltpu.VMEM((NZ, TB, QL), BF),
            dma((22,)),
            dma((NZ,)),
            dma((NZ,)),
            dma((NZ,)),
            dma((NZ,)),
            dma((6,)),
            dma((6,)),
            dma((3,)),
            dma((3,)),
            dma((4,)),
            dma((2 * NZ,)),
            dma((2 * NZ,)),
        ],
        compiler_params=pltpu.CompilerParams(
            collective_id=cid, has_side_effects=True, vmem_limit_bytes=62 * 2**20
        ),
    )(*tabs, tnat, tsm, comb)


def per_device(three_index, occ_blocks, virt_blocks, tile_shift, tile_count, block_owner):
    pos = lax.axis_index("pair")
    z = pos // 2 % NZ
    row_block, list_t, list_h, rank_at, rank_row, rank_src, rank_ok, block_place = tables(
        tile_shift, tile_count, block_owner
    )
    own_shift = lax.dynamic_index_in_dim(tile_shift, pos, 0, keepdims=False)
    own_count = lax.dynamic_index_in_dim(tile_count, pos, 0, keepdims=False)
    own_row = lax.dynamic_index_in_dim(row_block, pos, 0, keepdims=False)
    window = jnp.arange(W, dtype=jnp.int32)
    slot_of = jnp.sum(jnp.where(own_shift[None, :] == window[:, None], window[None, :], 0), axis=1)
    own_tab = jnp.concatenate(
        [block_place((own_row + window - 2) % RANKS), (slot_of < own_count).astype(jnp.int32), slot_of]
    )
    tabs = (
        lax.dynamic_index_in_dim(list_t, z, 0, keepdims=False),
        lax.dynamic_index_in_dim(list_h, z, 0, keepdims=False),
        rank_at,
        rank_row,
        rank_src,
        rank_ok,
        own_tab,
    )
    tsm = jnp.transpose(three_index, (2, 0, 1, 3))
    virt = jnp.transpose(virt_blocks[0], (1, 0, 2)).reshape(TB, 7 * TB)
    occ = jnp.transpose(occ_blocks[0], (1, 0, 2)).reshape(TB, 3 * TB)
    comb = jnp.concatenate([virt, jnp.zeros((TB, TB), BF), occ, jnp.zeros((TB, TB), BF)], axis=1)
    plane = jnp.max(jnp.sum(tile_count.reshape(NX, NZ, 2), axis=(0, 2)))
    return lax.cond(
        plane <= 20,
        functools.partial(fused, 20, 1),
        functools.partial(fused, 32, 2),
        tabs,
        three_index,
        tsm,
        comb,
    )


def solution(mesh):
    in_specs = (
        P("pair", None, None, "aux"),
        P("pair", None, None, None),
        P("pair", None, None, None),
        P(),
        P(),
        P(),
    )
    return jax.shard_map(per_device, mesh=mesh, in_specs=in_specs, out_specs=P("pair", "aux"), check_vma=False)
```

time: 615 us -> 263 us (0.43)
  blocking collectives: 292 us -> 0 us
  Pallas kernels: 0 us -> 239 us
  waiting for transfers between devices: 193 us -> 0 us
  local copies, waits for them, and re-layouts: 60.9 us -> 17.1 us
  matrix products: 38.4 us -> 0 us
  between operations: 13.7 us -> 0.83 us
  starting transfers between devices: 7.17 us -> 0 us
    pallas_call x0 -> x1, Pallas kernels: none -> 239 us  [fused(): pl.pallas_call(functools.partial(kernel, cap), out_shape=jax.ShapeDtypeSt...]
    psum x1 -> x0, waiting for transfers between devices: 193 us -> none  [per_device(): summed_all = lax.psum(partial_value, 'pair')]
    all_gather x2 -> x0, blocking collectives: 187 us -> none  [the longest x1 127 us: per_device(): lax.all_gather(occ_blocks, 'pair', axis=0, tiled=True)]
    all_to_all x1 -> x0, blocking collectives: 105 us -> none  [per_device(): lax.all_to_all(full_virt, 'pair', split_axis=0, concat_axis=2, tiled=True)]
    dot_general x5 -> x0, matrix products: 38.4 us -> none  [the longest x3 17.8 us: per_device(): jnp.einsum('tlm,tmx->tlx', occ_rows[:, neighbour], sources_flat[sources[:...]
    gather x20 -> x0, local copies, waits for them, and re-layouts: 28.1 us -> none  [the longest x3 14.9 us: per_device(): sources_flat[sources[:, neighbour]]]
    reshape x4, local copies, waits for them, and re-layouts: 20.9 us -> 1.06 us  [the longest x1 0.76 us: per_device(): plane = jnp.max(jnp.sum(tile_count.reshape(NX, NZ, 2), axis=(0, 2)))]
    all_to_all x1 -> x0, starting transfers between devices: 7.13 us -> none  [per_device(): lax.all_to_all(half_virt, 'pair', split_axis=2, concat_axis=0, tiled=True)]
  transfers between devices with their start and end apart: 3 -> 0, of which waited for: 1 -> 0; matrix products, arithmetic and copies ran while one was open for 14% -> 0% of each run, Pallas kernels for 0% -> 0%
where the time goes in v1:
time: 263 us
  Pallas kernels  239 us (91%)
  local copies, waits for them, and re-layouts  17.1 us (7%)
  other arithmetic  5.57 us (2%)
    pallas_call x1, Pallas kernels, fused(): pl.pallas_call(functools.partial(kernel, cap), out_shape=jax.ShapeDtypeSt...  239 us
    unnamed x3, local copies, waits for them, and re-layouts  7.86 us

profile of v1, /device:TPU:8, one launch (start us, length us, event | category | flops | bytes accessed | tf_op | source)
XLA Modules:
  0.0 263.1 jit_solution(18098958148801182724)
XLA Ops:
  0.0 1.2 dynamic_slice.22
  1.2 0.8 select_reduce_fusion.7
  2.0 0.7 dynamic_slice.20
  2.7 0.7 fusion.23
  3.4 0.9 dynamic-slice_reduce_fusion
  4.4 0.7 compare_convert_fusion
  5.4 0.8 reshape.332
  6.3 0.6 reduce_max.9
  7.9 0.2 multiply_reduce_fusion
  8.5 0.8 copy.60
  9.4 0.8 copy.56
  10.4 0.8 copy.59
  12.1 0.3 select_reduce_fusion.4
  12.4 0.2 fusion.14
  12.6 6.5 %copy.73 = bf16[4,32,32,512]{3,1,0,2:T(8,128)(2,1)} copy(bf16[4,32,32,512]{3,2,1,0:T(8,128)(2,1)} %param.8) | data formatting | bytes 8388608 | tf_op args[0]
  19.1 243.3 %conditional.1 = (f32[32,512]{1,0:T(8,128)S(1)}) conditional(s32[]{:T(128)} %convert_element_type.21, (pred[8,32,8,4]{1,3,2,0:T(4,128)(4,1)S(1)}, pred[8,32,8,4]{1,3,2,0:T(4,128)(4,1)S(1)}, s32[128]{0:T(128)S(1)}, pred[128]{0:T(512)(128)(4,1)S(1)}, pred[128,3]{0,1:T(4,128)(4,1)S(1)}, /*index=5*/pred[128,3]{0,1:T(4,128)(4,1)S(1)}, ...), branch_computations={%region_11.12_spmd.clone, %region_12.13_spmd.clone} | conditional | flops 36896 | bytes 87768 | solution.py:485
  19.3 0.6 multiply_add_fusion.1.rank_row
  20.0 0.1 copy.68
  20.5 0.2 select_reduce_fusion.2
  20.7 0.5 fusion.10
  21.3 0.8 reshape.339.rank_ok
  22.2 0.8 select_n.177.rank_src
  23.0 239.4 %branch_1_fun.1 = f32[32,512]{1,0:T(8,128)S(1)} custom-call(s32[32]{0:T(128)} %get-tuple-element.769.list_t, s32[32]{0:T(128)} %get-tuple-element.770.list_h, s32[128]{0:T(128)S(1)} %get-tuple-element.356, s32[128]{0:T(128)} %multiply_add_fusion.1.rank_row, s32[384]{0:T(512)} %select_n.177.rank_src, s32[384]{0:T(512)} %reshape.339.rank_ok, ...), custom_call_target="tpu_custom_call" | custom-call | tf_op jit(solution)/shard_map/cond/branch_1_fun/pallas_call | solution.py:411
  262.5 0.6 copy.77
  (54 shorter events, 3.1 us)

commit v2 on v1

v2 whole, which is shorter than its diff:
```python
import functools
import math

import jax
import jax.numpy as jnp
from jax import lax
from jax.experimental import pallas as pl
from jax.experimental.pallas import tpu as pltpu
from jax.sharding import PartitionSpec as P

NX, NY, NZ = 4, 4, 8
NG = 2 * NX
W = 4
TB = 32
HB = TB // 2
QL = 512
QH = QL // 2
LIVE = 128
RANKS = NG * NZ
OFF = (4, 3, 5, 2, 6, 1, 7, 0)
AHEAD = 2
CAPS = (20, 22, 24, 32)
MESH = pl.DeviceIdType.MESH
BF, F32 = jnp.bfloat16, jnp.float32


def fill_tables(pi, z, count, owner, shift, tab):
    tiles = RANKS * W

    def grid(lanes):
        return lax.broadcasted_iota(jnp.int32, (tiles, lanes), 0), lax.broadcasted_iota(jnp.int32, (tiles, lanes), 1)

    def pick(cond, value):
        return jnp.sum(jnp.where(cond, value, 0), axis=1, keepdims=True)

    def gather(cond, value):
        return jnp.sum(jnp.where(cond, value, 0), axis=0, keepdims=True)

    t, d = grid(RANKS)
    td = t // W
    zt, zd = td // 2 % NZ, d // 2 % NZ
    count_t = pick(d == td, count)
    before = pick((zd == zt) & (d < td), count)
    start = pick(zd < zt, count)
    row = pick(owner == td, d)
    tt, lane = grid(tiles)
    sub = lax.broadcasted_iota(jnp.int32, (RANKS, tiles), 0)
    at_lane = lax.broadcasted_iota(jnp.int32, (RANKS, tiles), 1)
    shift_r = jnp.zeros((1, tiles), jnp.int32)
    for jj in range(W):
        shift_r = shift_r + gather((at_lane // W == sub) & (at_lane % W == jj), shift[:, jj : jj + 1])
    shift_t = pick(tt == lane, shift_r)

    t, r = grid(128)
    j, td = t % W, t // W
    zt = td // 2 % NZ
    gt = 2 * (td // (2 * NZ)) + td % 2
    live = j < count_t
    place = before + j
    packed = zt * 32 + place
    key = row * W + shift_t
    by_rank = (start + place == r) & live
    rank_packed = gather(by_rank, packed)
    rank_key = gather(by_rank, key)
    mu, w = rank_key // W, rank_key % W

    def block_place(b):
        return (2 * (b // (2 * NZ)) + b % 2) * NZ + b // 2 % NZ

    tab[0:1, :] = rank_packed
    tab[1:2, :] = block_place(mu)
    for n in range(3):
        near_w = w + 1 - n
        near_key = ((mu + RANKS + n - 1) % RANKS) * W + near_w
        match = (key == near_key) & live & (near_w >= 0) & (near_w < W)
        found = gather(match, packed + 1)
        tab[2 + n : 3 + n, :] = jnp.where(found > 0, found - 1, rank_packed)
        tab[5 + n : 6 + n, :] = jnp.where(found > 0, 1, 0)
    in_plane = (zt == z) & live
    hit = in_plane & (place == r)
    tab[8:9, :] = gather(hit, gt * W + j)
    spare = r[0:1, :] >= gather(in_plane, 1)
    first = gather(in_plane & (place == 0), shift_t)
    tab[9:10, :] = gather(hit, gt * W + shift_t) + jnp.where(spare, first, 0)
    own = td == pi
    own_row = gather(own & (j == 0), row)
    tab[10:11, :] = block_place((own_row + RANKS + r[0:1, :] - 2) % RANKS)
    tab[11:12, :] = gather(own & live & (shift_t == r), 1)
    tab[12:13, :] = jnp.minimum(gather(own & (shift_t == r), j), W - 1)
    tab[13:16, :] = jnp.zeros((3, 128), jnp.int32)


def kernel(
    cap,
    count_v,
    owner_v,
    shift_v,
    virt_v,
    occ_v,
    tnat_h,
    out,
    tab_v,
    tab,
    tnat,
    ts,
    comb,
    hs,
    hbuf,
    txr0, txr1, txr2, txr3, txr4, txr5, txr6, txr7,
    hxr0, hxr1, hxr2, hxr3, hxr4, hxr5, hxr6, hxr7,
    tc,
    hc,
    tz,
    hz,
    at,
    fbuf,
    fout,
    pbuf,
    prx,
    rxs,
    rxr,
    rzs,
    rzr,
    sems,
    txr_s,
    tzr_s,
    hxr_s,
    hzr_s,
    ys_s,
    yr_s,
    cs_s,
    cr_s,
    loc_s,
    own_s,
    out_s,
    ps_s,
    pr_s,
    xs_s,
    xr_s,
):
    txr = (txr0, txr1, txr2, txr3, txr4, txr5, txr6, txr7)
    hxr = (hxr0, hxr1, hxr2, hxr3, hxr4, hxr5, hxr6, hxr7)
    pi = lax.axis_index("pair")
    y = lax.axis_index("aux")
    c = pi % 2
    z = pi // 2 % NZ
    x = pi // (2 * NZ)
    g = 2 * x + c

    def dev_g(gg):
        return ((gg // 2 * NZ + z) * 2 + gg % 2, y)

    def dev_z(zz):
        return ((x * NZ + zz) * 2 + c, y)

    yp, ym = (y + 1) % NY, (y + NY - 1) % NY
    core = dev_g(g + 1 - 2 * c)

    def remote(src, dst, send, recv, device):
        return pltpu.make_async_remote_copy(
            src_ref=src, dst_ref=dst, send_sem=send, recv_sem=recv, device_id=device, device_id_type=MESH
        )

    def wait_bytes(ref, sem):
        pltpu.make_async_copy(ref, ref, sem).wait()

    barrier = pltpu.get_barrier_semaphore()
    for i in range(1, NG):
        pl.semaphore_signal(barrier, inc=1, device_id=dev_g((g + i) % NG), device_id_type=MESH)
    for i in range(1, NZ):
        pl.semaphore_signal(barrier, inc=1, device_id=dev_z((z + i) % NZ), device_id_type=MESH)
    pl.semaphore_signal(barrier, inc=1, device_id=(pi, yp), device_id_type=MESH)
    pl.semaphore_signal(barrier, inc=1, device_id=(pi, ym), device_id_type=MESH)

    own_t, own_h = [], []
    nat = pltpu.make_async_copy(tnat_h, tnat, loc_s.at[1])
    nat.start()
    gap = jnp.zeros((TB, TB), BF)
    blocks = [virt_v[0, i] for i in range(7)] + [gap] + [occ_v[0, i] for i in range(3)] + [gap]
    comb[g * NZ + z] = jnp.concatenate(blocks, axis=1)
    nat.wait()

    def split(st):
        @pl.loop(0, W)
        def _(j):
            for mh in range(2):
                for q in range(0, QL, 128):
                    part = tnat[j, mh * HB : (mh + 1) * HB, pl.ds(pl.multiple_of(st * HB, HB), HB), q : q + 128]
                    part = jnp.swapaxes(part.astype(F32), 0, 1).astype(BF)
                    ts[pl.ds(st * HB, HB), j, mh * HB : (mh + 1) * HB, q : q + 128] = part

    first = (z + OFF[0]) % NZ // (NZ // 2)
    split(first)
    pl.semaphore_wait(barrier, NG + NZ)

    for i in range(1, NZ):
        remote(comb.at[g * NZ + z], comb.at[g * NZ + z], cs_s.at[0], cr_s.at[0], dev_z((z + i) % NZ)).start()

    def t_send(k):
        zb = (z + OFF[k]) % NZ
        own_t.append(
            pltpu.make_async_copy(
                ts.at[zb * NX + x, :, pl.ds(HB * c, HB), :], txr[k].at[pl.ds(W * g, W)], own_s.at[k]
            )
        )
        own_t[k].start()
        for i in range(1, NG):
            gg = (g + i) % NG
            remote(
                ts.at[zb * NX + gg // 2, :, pl.ds(HB * (gg % 2), HB), :],
                txr[k].at[pl.ds(W * g, W)],
                out_s.at[k],
                txr_s.at[k],
                dev_g(gg),
            ).start()

    t_send(0)
    split(1 - first)
    for k in range(1, AHEAD):
        t_send(k)

    fill_tables(pi, z, count_v[...], owner_v[...], shift_v[...], tab_v)
    tab_c = pltpu.make_async_copy(tab_v, tab, loc_s.at[0])
    tab_c.start()
    tab_c.wait()

    def t_step(k):
        zb = (z + OFF[k]) % NZ
        own_t[k].wait()
        wait_bytes(txr[k].at[pl.ds(0, (NG - 1) * W)], txr_s.at[k])
        if k + AHEAD < NZ:
            t_send(k + AHEAD)
        if OFF[k] == 0:

            @pl.loop(0, cap)
            def _(i):
                tz[z, i] = txr[k][tab[8, i]]

        else:

            @pl.loop(0, cap)
            def _(i):
                tc[zb, i] = txr[k][tab[8, i]]

            remote(tc.at[zb], tz.at[z], sems.at[1], tzr_s.at[z], dev_z(zb)).start()

    t_step(0)
    wait_bytes(comb.at[pl.ds(0, NZ - 1)], cr_s.at[0])
    for i in range(1, NX):
        remote(
            comb.at[pl.ds(g * NZ, NZ)], comb.at[pl.ds(g * NZ, NZ)], cs_s.at[1], cr_s.at[1], dev_g((g + 2 * i) % NG)
        ).start()
    remote(comb.at[pl.ds(g * NZ, NZ)], comb.at[pl.ds(g * NZ, NZ)], cs_s.at[1], cr_s.at[1], core).start()
    t_step(1)
    wait_bytes(comb.at[pl.ds(0, NX * NZ)], cr_s.at[1])
    for i in range(1, NX):
        gg = (g + 2 * i) % NG
        remote(comb.at[pl.ds(gg * NZ, NZ)], comb.at[pl.ds(gg * NZ, NZ)], cs_s.at[2], cr_s.at[2], core).start()
    t_step(2)

    wait_bytes(comb.at[pl.ds(0, (NX - 1) * NZ)], cr_s.at[2])
    lane = lax.broadcasted_iota(jnp.int32, (TB, W * TB), 1) // TB
    keep = lane < 0
    for kk in range(W):
        keep = keep | ((lane == kk) & (tab[11, kk] > 0))
    rows = []
    for ww in range(W):
        band = comb[tab[10, ww], :, 0:256].astype(F32)
        band = pltpu.roll(band, (256 - TB * (W - 1 - ww)) % 256, 1)[:, : W * TB]
        rows.append(jnp.where(keep, band, 0.0).astype(BF))
    vmat = jnp.concatenate(rows, axis=0)
    slots = [tab[12, ww] for ww in range(W)]

    def h_form(qh, mh):
        @pl.loop(0, HB)
        def _(mi):
            rhs = jnp.concatenate(
                [tnat[slots[ww], mh * HB + mi, :, qh * QH : (qh + 1) * QH] for ww in range(W)], axis=0
            )
            hs[mi] = jnp.dot(vmat, rhs, preferred_element_type=F32)

        for ww in range(W):

            @pl.loop(0, TB // 8)
            def _(sb):
                part = hs[:, pl.ds(ww * TB + sb * 8, 8), :]
                hbuf[qh, pl.ds(sb * 8, 8), ww, mh * HB : (mh + 1) * HB, :] = jnp.swapaxes(part, 0, 1).astype(BF)

    for i in range(4):
        h_form(i // 2, i % 2)
        t_step(3 + i)

    def h_send(k):
        zb = (z + OFF[k]) % NZ
        own_h.append(pltpu.make_async_copy(hbuf.at[c, zb * NX + x], hxr[k].at[pl.ds(W * g, W)], own_s.at[NZ + k]))
        own_h[k].start()
        for i in range(1, NG):
            gg = (g + i) % NG
            remote(
                hbuf.at[gg % 2, zb * NX + gg // 2], hxr[k].at[pl.ds(W * g, W)], out_s.at[NZ + k], hxr_s.at[k], dev_g(gg)
            ).start()

    h_send(0)
    t_step(7)
    for k in range(1, AHEAD):
        h_send(k)

    def h_step(k):
        zb = (z + OFF[k]) % NZ
        own_h[k].wait()
        wait_bytes(hxr[k].at[pl.ds(0, (NG - 1) * W)], hxr_s.at[k])
        if k + AHEAD < NZ:
            h_send(k + AHEAD)
        if OFF[k] == 0:

            @pl.loop(0, cap)
            def _(i):
                hz[z, i] = hxr[k][tab[9, i]]

        else:

            @pl.loop(0, cap)
            def _(i):
                hc[zb, i] = hxr[k][tab[9, i]]

            remote(hc.at[zb], hz.at[z], sems.at[3], hzr_s.at[z], dev_z(zb)).start()

    h_step(0)
    h_step(1)

    for i in range(1, NZ):
        zz = (z + i) % NZ
        wait_bytes(tz.at[zz], tzr_s.at[zz])

    @pl.loop(0, LIVE // 8)
    def _(b):
        tiles = []
        for i in range(8):
            p = tab[0, b * 8 + i]
            tiles.append(tz[p // 32, p % 32])
        at[y, :, pl.ds(b * 128, 128)] = jnp.concatenate(tiles, axis=0).T

    lo, hi = pl.ds(0, QH), pl.ds(QH, QH)
    remote(at.at[y, lo], at.at[y, lo], ys_s.at[0], yr_s.at[0], (pi, yp)).start()
    remote(at.at[y, hi], at.at[y, hi], ys_s.at[1], yr_s.at[1], (pi, ym)).start()
    remote(at.at[y, hi], at.at[y, hi], ys_s.at[2], yr_s.at[2], (pi, yp)).start()
    remote(at.at[y, lo], at.at[y, lo], ys_s.at[3], yr_s.at[3], (pi, ym)).start()

    for k in range(2, 6):
        h_step(k)
    wait_bytes(at.at[ym, lo], yr_s.at[0])
    remote(at.at[ym, lo], at.at[ym, lo], ys_s.at[4], yr_s.at[4], (pi, yp)).start()
    wait_bytes(at.at[yp, hi], yr_s.at[1])
    remote(at.at[yp, hi], at.at[yp, hi], ys_s.at[5], yr_s.at[5], (pi, ym)).start()
    for k in range(6, NZ):
        h_step(k)

    for i in range(1, NZ):
        zz = (z + i) % NZ
        wait_bytes(hz.at[zz], hzr_s.at[zz])
    lane3 = lax.broadcasted_iota(jnp.int32, (TB, 3 * TB), 1) // TB

    @pl.loop(0, LIVE)
    def _(t):
        occ = comb[tab[1, t], :, 256 : 256 + 3 * TB]
        src, use = [], lane3 < 0
        for r in range(3):
            p = tab[2 + r, t]
            src.append(hz[p // 32, p % 32])
            use = use | ((lane3 == r) & (tab[5 + r, t] > 0))
        occ = jnp.where(use, occ.astype(F32), 0.0).astype(BF)
        f = jnp.dot(occ, jnp.concatenate(src, axis=0), preferred_element_type=F32).astype(BF)
        lower = c == 0
        fbuf[c, t] = jnp.where(lower, f[:HB], f[HB:])
        fout[t] = jnp.where(lower, f[HB:], f[:HB])

    swap = remote(fout, fbuf.at[c], sems.at[4], sems.at[5], core)
    swap.start()
    for i, ref in ((2, at.at[ym, hi]), (3, at.at[yp, lo]), (4, at.at[(y + 2) % NY, lo]), (5, at.at[(y + 2) % NY, hi])):
        wait_bytes(ref, yr_s.at[i])
    swap.wait_recv()

    def core_sum(h, i):
        xb = (x + 1 + i) % NX
        wait_bytes(prx.at[h, i], pr_s.at[NX * h + i])
        return pbuf[h, xb, :, c] + prx[h, i]

    def ship(h, i):
        xb = (x + 1 + i) % NX
        rxs[h, i] = core_sum(h, i).astype(BF)
        remote(rxs.at[h, i], rxr.at[h, i], xs_s.at[NX * h + i], xr_s.at[NX * h + i], dev_g(2 * xb + c)).start()

    for h in range(2):
        for i in range(NX):
            xb = (x + 1 + i) % NX

            @pl.loop(0, 4)
            def _(mt):
                term = jnp.dot(
                    at[xb, pl.ds(mt * 128, 128), :],
                    fbuf[h].reshape(LIVE * HB, QH),
                    preferred_element_type=F32,
                )
                pbuf[h, xb, pl.ds(mt * 2, 2)] = term.reshape(2, 2, TB, QH)

            remote(pbuf.at[h, xb, :, 1 - c], prx.at[h, i], ps_s.at[NX * h + i], pr_s.at[NX * h + i], core).start()
            if i > 0:
                ship(h, i - 1)

    for h in range(2):
        total = core_sum(h, NX - 1)
        for i in range(NX - 1):
            wait_bytes(rxr.at[h, i], xr_s.at[NX * h + i])
            total = total + rxr[h, i].astype(F32)
        rzs[h] = total.astype(BF)
        for i in range(1, NZ):
            zz = (z + i) % NZ
            remote(rzs.at[h, zz], rzr.at[h, z], sems.at[6 + h], sems.at[8 + h], dev_z(zz)).start()
        rzr[h, z] = rzs[h, z]
    for h in range(2):
        wait_bytes(rzs.at[h, pl.ds(0, NZ - 1)], sems.at[8 + h])
        final = rzr[h, 0].astype(F32)
        for zz in range(1, NZ):
            final = final + rzr[h, zz].astype(F32)
        out[:, h * QH : (h + 1) * QH] = final * (1.0 / math.sqrt(TB * TB * LIVE))

    wait_bytes(comb.at[pl.ds(0, NZ - 1)], cs_s.at[0])
    wait_bytes(comb.at[pl.ds(0, NX * NZ)], cs_s.at[1])
    wait_bytes(comb.at[pl.ds(0, (NX - 1) * NZ)], cs_s.at[2])
    for k in range(NZ):
        wait_bytes(txr[k].at[pl.ds(0, (NG - 1) * W)], out_s.at[k])
    wait_bytes(tc.at[pl.ds(0, NZ - 1)], sems.at[1])
    for k in range(NZ):
        wait_bytes(hxr[k].at[pl.ds(0, (NG - 1) * W)], out_s.at[NZ + k])
    wait_bytes(hc.at[pl.ds(0, NZ - 1)], sems.at[3])
    swap.wait_send()
    for i in range(6):
        wait_bytes(at.at[y, lo], ys_s.at[i])
    for h in range(2):
        wait_bytes(rzs.at[h, pl.ds(0, NZ - 1)], sems.at[6 + h])
        for i in range(NX - 1):
            wait_bytes(rxs.at[h, i], xs_s.at[NX * h + i])
        for i in range(NX):
            wait_bytes(prx.at[h, i], ps_s.at[NX * h + i])


def fused(cap, cid, *operands):
    vmem = pl.BlockSpec(memory_space=pltpu.VMEM)
    hbm = pl.BlockSpec(memory_space=pl.ANY)
    dma = pltpu.SemaphoreType.DMA
    return pl.pallas_call(
        functools.partial(kernel, cap),
        out_shape=jax.ShapeDtypeStruct((TB, QL), F32),
        in_specs=[vmem] * 5 + [hbm],
        out_specs=vmem,
        scratch_shapes=[
            pltpu.VMEM((16, 128), jnp.int32),
            pltpu.SMEM((16, 128), jnp.int32),
            pltpu.VMEM((W, TB, TB, QL), BF),
            pltpu.VMEM((TB, W, TB, QL), BF),
            pltpu.VMEM((RANKS, TB, 384), BF),
            pltpu.VMEM((HB, W * TB, QH), F32),
            pltpu.VMEM((2, TB, W, TB, QH), BF),
        ]
        + [pltpu.VMEM((NG * W, HB, QL), BF)] * NZ
        + [pltpu.VMEM((NG * W, TB, QH), BF)] * NZ
        + [
            pltpu.VMEM((NZ, cap, HB, QL), BF),
            pltpu.VMEM((NZ, cap, TB, QH), BF),
            pltpu.VMEM((NZ, cap, HB, QL), BF),
            pltpu.VMEM((NZ, cap, TB, QH), BF),
            pltpu.VMEM((NY, QL, LIVE * HB), BF),
            pltpu.VMEM((2, LIVE, HB, QH), BF),
            pltpu.VMEM((LIVE, HB, QH), BF),
            pltpu.VMEM((2, NX, NZ, 2, TB, QH), F32),
            pltpu.VMEM((2, NX, NZ, TB, QH), F32),
            pltpu.VMEM((2, NX - 1, NZ, TB, QH), BF),
            pltpu.VMEM((2, NX - 1, NZ, TB, QH), BF),
            pltpu.VMEM((2, NZ, TB, QH), BF),
            pltpu.VMEM((2, NZ, TB, QH), BF),
            dma((10,)),
            dma((NZ,)),
            dma((NZ,)),
            dma((NZ,)),
            dma((NZ,)),
            dma((6,)),
            dma((6,)),
            dma((3,)),
            dma((3,)),
            dma((4,)),
            dma((2 * NZ,)),
            dma((2 * NZ,)),
            dma((2 * NX,)),
            dma((2 * NX,)),
            dma((2 * NX,)),
            dma((2 * NX,)),
        ],
        compiler_params=pltpu.CompilerParams(
            collective_id=cid, has_side_effects=True, vmem_limit_bytes=62 * 2**20
        ),
    )(*operands)


def per_device(three_index, occ_blocks, virt_blocks, tile_shift, tile_count, block_owner):
    plane = jnp.max(jnp.sum(tile_count.reshape(NX, NZ, 2), axis=(0, 2)))
    need = jnp.sum(jnp.stack([plane > cap for cap in CAPS[:-1]]).astype(jnp.int32))
    return lax.switch(
        need,
        [functools.partial(fused, cap, 1 + i) for i, cap in enumerate(CAPS)],
        tile_count.reshape(1, RANKS),
        block_owner.reshape(1, RANKS),
        tile_shift,
        virt_blocks,
        occ_blocks,
        three_index,
    )


def solution(mesh):
    in_specs = (
        P("pair", None, None, "aux"),
        P("pair", None, None, None),
        P("pair", None, None, None),
        P(),
        P(),
        P(),
    )
    return jax.shard_map(per_device, mesh=mesh, in_specs=in_specs, out_specs=P("pair", "aux"), check_vma=False)
```

time: 263 us -> 198 us (0.75)
  Pallas kernels: 239 us -> 190 us
  local copies, waits for them, and re-layouts: 17.1 us -> 2.77 us
  other arithmetic: 5.57 us -> 1.47 us
    pallas_call x1, Pallas kernels: 239 us -> 190 us  [fused(): pl.pallas_call(functools.partial(kernel, cap), out_shape=jax.ShapeDtypeSt...]
    unnamed x3 -> x1, local copies, waits for them, and re-layouts: 7.86 us -> 0.63 us
    dynamic_slice x3 -> x0, local copies, waits for them, and re-layouts: 2.78 us -> none  [the longest x1 1.24 us: per_device(): own_count = lax.dynamic_index_in_dim(tile_count, pos, 0, keepdims=False)]
where the time goes in v2:
time: 198 us
  Pallas kernels  190 us (96%)
  local copies, waits for them, and re-layouts  2.77 us (1%)
  between operations  2.62 us (1%)
    pallas_call x1, Pallas kernels, fused(): pl.pallas_call(functools.partial(kernel, cap), out_shape=jax.ShapeDtypeSt...  190 us

profile of v2, /device:TPU:8, one launch (start us, length us, event | category | flops | bytes accessed | tf_op | source)
XLA Modules:
  0.0 197.7 jit_solution(10618476541244800288)
XLA Ops:
  0.0 0.7 reshape.9
  0.8 0.1 reduce_sum.18
  0.9 0.6 reduce_max.9
  3.5 0.7 fusion
  4.8 192.3 %conditional.1 = (f32[32,512]{1,0:T(8,128)S(1)}) conditional(s32[]{:T(128)} %clamp.3, (s32[64]{0:T(128)}, s32[64]{0:T(128)}, s32[64,4]{0,1:T(4,128)}, bf16[1,7,32,32]{3,2,1,0:T(8,128)(2,1)}, bf16[1,3,32,32]{3,2,1,0:T(8,128)(2,1)}, /*index=5*/bf16[4,32,32,512]{3,2,1,0:T(8,128)(2,1)}) %tuple.17, (s32[64]{0:T(128)}, ...), branch_computations={%region_3.0_spmd, %region_4.0_spmd, %region_5.0_spmd, %region_6.0_... | conditional | bytes 2056 | solution.py:507
  5.0 1.4 copy.36.shift_v
  6.4 190.2 %branch_1_fun.1 = f32[32,512]{1,0:T(8,128)S(1)} custom-call(s32[1,64]{1,0:T(1,128)} %bitcast.12, s32[1,64]{1,0:T(1,128)} %bitcast.16, s32[64,4]{1,0:T(8,128)} %copy.36.shift_v, bf16[1,7,32,32]{3,2,1,0:T(8,128)(2,1)} %get-tuple-element.116.virt_v, bf16[1,3,32,32]{3,2,1,0:T(8,128)(2,1)} %get-tuple-element.120.occ_v, ...), custom_call_target="tpu_custom_call" | custom-call | tf_op jit(solution)/shard_map/cond/branch_1_fun/pallas_call | solution.py:451
  197.1 0.6 copy.44
